TPU v7x, 256 devices: a whole 4x4x8 slice. The times are simulated.
256 devices in a mesh: wide: 16 (over x, y), narrow: 16 (over z, core).
Axes of the slice: x: 4, y: 4, z: 8, core: 2. Of those that a mesh axis runs over, the one named last changes fastest.
Arguments:
- entries: int32 [65536, 32, 256], P(('wide', 'narrow')), may hold values from 0 to 2
- factor_a: float32 [131072, 128], P(('wide', 'narrow')), may hold values from -4.2 to 4.2
- factor_b: float32 [131072, 128], P(('wide', 'narrow')), may hold values from -4.2 to 4.2
- factor_c: float32 [8192, 128], P('wide'), may hold values from -4.2 to 4.2
- index_a: int32 [65536], P(('wide', 'narrow')), may hold values from 0 to 511
- index_b: int32 [65536], P(('wide', 'narrow')), may hold values from 0 to 511
- index_c: int32 [8192], P(('wide', 'narrow')), may hold values from 0 to 511
Outputs:
- step_a: float32 [131072, 128], P(('wide', 'narrow'))
- step_b: float32 [131072, 128], P(('wide', 'narrow'))
- step_c: float32 [8192, 128], P('wide')
All inputs are finite; a program needn't handle non-finite values.
Results may differ from a plain program's by a relative error of at most 0.0048.
Values may be sent and summed in bfloat16 or wider, within the bound.
No kernel may reach another device: no remote copies, remote signals or barrier semaphores. Data moves between devices by JAX's collectives and lax.ppermute only.
A program may use at most 128 MiB of HBM per device.

v0:
```python
import jax
import jax.numpy as jnp
from jax import lax
from jax.sharding import PartitionSpec as P

CG_ITERS = 2
ridge_weight = 25.0


def outer_pairs(rows_first, rows_third):
    product = (
        rows_first.astype(jnp.float32)[:, None, :] * rows_third.astype(jnp.float32)[None, :, :]
    )
    return product.astype(jnp.bfloat16).reshape(-1, rows_first.shape[1])


def model_values(pairs, rows_second):
    return lax.dot_general(
        pairs, rows_second, (((1,), (1,)), ((), ())), preferred_element_type=jnp.float32
    )


def fisher_terms(model, codes):
    sampled = (codes > 0).astype(jnp.float32)
    present = (codes == 2).astype(jnp.float32)
    prob = jax.nn.sigmoid(model)
    weight = sampled * prob * (1.0 - prob)
    slope = (sampled * (prob - present)).astype(jnp.bfloat16)
    return (weight, slope)


def transposed(upstream, pairs, rows_first, rows_second, rows_third):
    over = jnp.dot(upstream, rows_second, preferred_element_type=jnp.float32)
    over = over.reshape(rows_first.shape[0], rows_third.shape[0], -1)
    to_first = jnp.sum(over * rows_third.astype(jnp.float32)[None, :, :], axis=1)
    to_third = jnp.sum(over * rows_first.astype(jnp.float32)[:, None, :], axis=0)
    to_second = lax.dot_general(
        upstream, pairs, (((0,), (0,)), ((), ())), preferred_element_type=jnp.float32
    )
    return (to_first, to_second, to_third)


def add_scaled(base_set, factor, extra_set):
    return (
        base_set[0] + factor * extra_set[0],
        base_set[1] + factor * extra_set[1],
        base_set[2] + factor * extra_set[2],
    )


def local(entries, factor_a, factor_b, factor_c, index_a, index_b, index_c):
    wide_count = lax.axis_size("wide")
    narrow_count = lax.axis_size("narrow")
    block_first, block_third, block_second = entries.shape
    slots_a = block_first // wide_count
    slots_b = block_second // narrow_count
    slots_c = block_third // wide_count
    codes = entries.reshape(block_first * block_third, block_second)
    c_weight = (lax.axis_index("narrow") == 0).astype(jnp.float32)

    def tube_total(partial_value):
        return lax.psum(partial_value, "narrow")

    def fetch(table_a, table_b, table_c):
        send_a = table_a[index_a].astype(jnp.bfloat16).reshape(wide_count, slots_a, -1)
        send_c = table_c[index_c].astype(jnp.bfloat16).reshape(wide_count, slots_c, -1)
        got_a, got_c = (
            lax.all_to_all(send_a, "wide", split_axis=0, concat_axis=0, tiled=True),
            lax.all_to_all(send_c, "wide", split_axis=0, concat_axis=0, tiled=True),
        )
        send_b = table_b[index_b].astype(jnp.bfloat16).reshape(narrow_count, slots_b, -1)
        got_b = lax.all_to_all(send_b, "narrow", split_axis=0, concat_axis=0, tiled=True)
        return (
            got_a.reshape(block_first, -1),
            got_b.reshape(block_second, -1),
            got_c.reshape(block_third, -1),
        )

    def give_back(parts, field):
        back_a, back_c = (
            lax.all_to_all(
                parts[0].reshape(wide_count, slots_a, -1),
                "wide",
                split_axis=0,
                concat_axis=0,
                tiled=True,
            ),
            lax.all_to_all(
                parts[2].reshape(wide_count, slots_c, -1),
                "wide",
                split_axis=0,
                concat_axis=0,
                tiled=True,
            ),
        )
        back_b = lax.all_to_all(
            parts[1].reshape(narrow_count, slots_b, -1),
            "narrow",
            split_axis=0,
            concat_axis=0,
            tiled=True,
        )
        sum_a = (
            jnp.zeros(factor_a.shape, jnp.float32).at[index_a].add(back_a.reshape(block_first, -1))
        )
        sum_b = (
            jnp.zeros(factor_b.shape, jnp.float32).at[index_b].add(back_b.reshape(block_second, -1))
        )
        part_c = (
            jnp.zeros(factor_c.shape, jnp.float32).at[index_c].add(back_c.reshape(block_third, -1))
        )
        sum_c = tube_total(part_c)
        return (
            sum_a + ridge_weight * field[0],
            sum_b + ridge_weight * field[1],
            sum_c + ridge_weight * field[2],
        )

    rows_first, rows_second, rows_third = fetch(factor_a, factor_b, factor_c)
    pairs = outer_pairs(rows_first, rows_third)
    weight, slope = fisher_terms(model_values(pairs, rows_second), codes)
    gradient = give_back(
        transposed(slope, pairs, rows_first, rows_second, rows_third),
        (factor_a, factor_b, factor_c),
    )

    def local_inner(first_set, second_set):
        return (
            jnp.sum(first_set[0] * second_set[0])
            + jnp.sum(first_set[1] * second_set[1])
            + c_weight * jnp.sum(first_set[2] * second_set[2])
        )

    def squares(vector_set):
        return lax.psum(local_inner(vector_set, vector_set), ("wide", "narrow"))

    solution = (
        jnp.zeros_like(gradient[0]),
        jnp.zeros_like(gradient[1]),
        jnp.zeros_like(gradient[2]),
    )
    residual = add_scaled(solution, -1.0, gradient)
    direction = residual
    norm_now = squares(residual)
    for iteration in range(CG_ITERS):
        d_first, d_second, d_third = fetch(direction[0], direction[1], direction[2])
        mixed = d_first.astype(jnp.float32)[:, None, :] * rows_third.astype(jnp.float32)[None, :, :]
        mixed = (
            mixed
            + rows_first.astype(jnp.float32)[:, None, :] * d_third.astype(jnp.float32)[None, :, :]
        )
        mixed = mixed.astype(jnp.bfloat16).reshape(block_first * block_third, -1)
        change = model_values(mixed, rows_second) + model_values(pairs, d_second)
        scaled = (weight * change).astype(jnp.bfloat16)
        image = give_back(transposed(scaled, pairs, rows_first, rows_second, rows_third), direction)
        alpha = norm_now / lax.psum(local_inner(direction, image), ("wide", "narrow"))
        solution = add_scaled(solution, alpha, direction)
        residual = add_scaled(residual, -alpha, image)
        if iteration + 1 < CG_ITERS:
            norm_next = squares(residual)
            direction = add_scaled(residual, norm_next / norm_now, direction)
            norm_now = norm_next
    return (solution[0], solution[1], solution[2])


def solution(mesh):
    placed = (
        P(("wide", "narrow"), None, None),
        P(("wide", "narrow"), None),
        P(("wide", "narrow"), None),
        P("wide", None),
        P(("wide", "narrow")),
        P(("wide", "narrow")),
        P(("wide", "narrow")),
    )
    return jax.shard_map(
        local,
        mesh=mesh,
        in_specs=placed,
        out_specs=(P(("wide", "narrow"), None), P(("wide", "narrow"), None), P("wide", None)),
        check_vma=False,
    )
```

profile of v0, /device:TPU:1, one launch (start us, length us, event | category | flops | bytes accessed | tf_op | source)
XLA Modules:
  0.0 847.4 jit_solution(3459871042274869847)
XLA Ops:
  10.0 7.6 all-to-all-start.1
  18.9 7.4 broadcast_compare_fusion
  27.7 6.7 all-to-all-start
  40.9 11.1 %all-to-all-start.2 = ((bf16[16,16,128]{2,1,0:T(8,128)(2,1)}), bf16[16,16,128]{2,1,0:T(8,128)(2,1)S(1)}, u32[]{:S(2)}, u32[]{:S(2)}) async-start(bf16[16,16,128]{2,1,0:T(8,128)(2,1)} %bitcast.6), calls=%async_computation.2 | async-start | bytes 131072 | tf_op jit(solution)/shard_map/all_to_all | solution.py:72
  59.8 8.6 %subtract_multiply_fusion = (f32[8192,256]{1,0:T(8,128)}, bf16[8192,256]{1,0:T(8,128)(2,1)S(1)}) fusion(pred[256,32,256]{2,1,0:T(32,128)(4,1)} %get-tuple-element.25, f32[256,32,256]{2,1,0:T(8,128)} %get-tuple-element.26, bf16[8192,128]{1,0:T(8,128)(2,1)S(1)} %bitcast.86, bf16[256,128]{1,0:T(8,128)(2,1)S(1)} %bitcast.103), kind=kOutput, calls=%fused_computation.31 | convolution fusion | flops 555745280 | bytes 25231360 | tf_op jit(solution)/shard_map/dot_general | solution.py:18
  77.7 6.3 all-to-all-done.5
  89.6 6.4 copy.18
  98.0 99.5 %all-reduce.5.cloned.1.call-done = f32[512,128]{1,0:T(8,128)} async-done(((f32[512,128]{1,0:T(8,128)}), f32[512,128]{1,0:T(8,128)}) %all-reduce.5.cloned.1.call-update) | async-done | bytes 262160 | tf_op jit(solution)/shard_map/psum | solution.py:62
  199.7 6.5 all-to-all-start.7
  222.5 9.3 %all-to-all-start.4 = ((f32[16,16,128]{2,1,0:T(8,128)}), f32[16,16,128]{2,1,0:T(8,128)S(1)}, u32[]{:S(2)}, u32[]{:S(2)}) async-start(f32[16,16,128]{2,1,0:T(8,128)} %fusion.21), calls=%async_computation.4 | async-start | bytes 262144 | tf_op jit(solution)/shard_map/all_to_all | solution.py:96
  255.6 7.0 fusion.4
  271.9 6.4 copy.21
  278.2 6.6 all-to-all-start.9
  292.3 7.6 all-to-all-start.10
  302.3 97.3 %all-reduce.7.cloned.1.call-done = f32[512,128]{1,0:T(8,128)} async-done(((f32[512,128]{1,0:T(8,128)}), f32[512,128]{1,0:T(8,128)}) %all-reduce.7.cloned.1.call-update) | async-done | bytes 262160 | tf_op jit(solution)/shard_map/psum | solution.py:62
  408.3 77.7 %all-reduce = (f32[]{:T(128)}, f32[]{:T(128)}) all-reduce(f32[]{:T(128)S(6)} %add.165, f32[]{:T(128)S(6)} %add.170), channel_id=1, replica_groups=mesh['wide'=16,'narrow'=16] {'wide','narrow'}, use_global_device_ids=true, to_apply=%region_9.0 | all-reduce | flops 2 | bytes 16 | tf_op jit(solution)/shard_map/psum | solution.py:135
  492.2 72.2 %psum.53 = f32[]{:T(128)} all-reduce(f32[]{:T(128)S(6)} %add.175), channel_id=1, replica_groups=mesh['wide'=16,'narrow'=16] {'wide','narrow'}, use_global_device_ids=true, to_apply=%region_23.0 | all-reduce | flops 1 | bytes 8 | tf_op jit(solution)/shard_map/psum | solution.py:135
  590.8 7.9 all-to-all-start.14
  606.7 7.0 fusion.5
  623.2 6.4 copy.24
  629.6 6.6 all-to-all-start.15
  643.0 9.1 %all-to-all-start.16 = ((f32[16,16,128]{2,1,0:T(8,128)}), f32[16,16,128]{2,1,0:T(8,128)S(1)}, u32[]{:S(2)}, u32[]{:S(2)}) async-start(f32[16,16,128]{2,1,0:T(8,128)} %fusion.25), calls=%async_computation.16 | async-start | bytes 262144 | tf_op jit(solution)/shard_map/all_to_all | solution.py:96
  654.9 98.0 %all-reduce.9.cloned.1.call-done = f32[512,128]{1,0:T(8,128)} async-done(((f32[512,128]{1,0:T(8,128)}), f32[512,128]{1,0:T(8,128)}) %all-reduce.9.cloned.1.call-update) | async-done | bytes 262160 | tf_op jit(solution)/shard_map/psum | solution.py:62
  759.2 77.7 %psum.55 = f32[]{:T(128)} all-reduce(f32[]{:T(128)S(6)} %add.183), channel_id=1, replica_groups=mesh['wide'=16,'narrow'=16] {'wide','narrow'}, use_global_device_ids=true, to_apply=%region_33.0 | all-reduce | flops 1 | bytes 8 | tf_op jit(solution)/shard_map/psum | solution.py:156
  (144 shorter events, 164.2 us)
Async XLA Ops:
  10.0 17.7 %all-to-all-start.1 = ((bf16[16,2,128]{2,1,0:T(2,128)(2,1)}), bf16[16,2,128]{2,1,0:T(2,128)(2,1)S(1)}, u32[]{:S(2)}, u32[]{:S(2)}) async-start(bf16[16,2,128]{2,1,0:T(2,128)(2,1)} %bitcast.3), calls=%async_computation.1 | async-start | bytes 16384 | tf_op jit(solution)/shard_map/all_to_all | solution.py:69
  27.7 13.2 %all-to-all-start = ((bf16[16,16,128]{2,1,0:T(8,128)(2,1)}), bf16[16,16,128]{2,1,0:T(8,128)(2,1)S(1)}, u32[]{:S(2)}, u32[]{:S(2)}) async-start(bf16[16,16,128]{2,1,0:T(8,128)(2,1)} %bitcast.1), calls=%async_computation | async-start | bytes 131072 | tf_op jit(solution)/shard_map/all_to_all | solution.py:68
  40.9 19.0 %all-to-all-start.2 = ((bf16[16,16,128]{2,1,0:T(8,128)(2,1)}), bf16[16,16,128]{2,1,0:T(8,128)(2,1)S(1)}, u32[]{:S(2)}, u32[]{:S(2)}) async-start(bf16[16,16,128]{2,1,0:T(8,128)(2,1)} %bitcast.6), calls=%async_computation.2 | async-start | bytes 131072 | tf_op jit(solution)/shard_map/all_to_all | solution.py:72
  59.8 202.8 %copy-start.10 = (bf16[16,16,128]{2,1,0:T(8,128)(2,1)}, bf16[16,16,128]{2,1,0:T(8,128)(2,1)S(1)}, u32[]{:S(2)}) copy-start(bf16[16,16,128]{2,1,0:T(8,128)(2,1)S(1)} %all-to-all-done.2) | copy-start | bytes 196612
  74.1 9.9 %all-to-all-start.5 = ((f32[16,2,128]{2,1,0:T(2,128)}), f32[16,2,128]{2,1,0:T(2,128)S(1)}, u32[]{:S(2)}, u32[]{:S(2)}) async-start(f32[16,2,128]{2,1,0:T(2,128)} %bitcast.17), calls=%async_computation.5 | async-start | bytes 32768 | tf_op jit(solution)/shard_map/all_to_all | solution.py:88
  84.0 11.9 %all-to-all-start.3 = ((f32[16,16,128]{2,1,0:T(8,128)}), f32[16,16,128]{2,1,0:T(8,128)S(1)}, u32[]{:S(2)}, u32[]{:S(2)}) async-start(f32[16,16,128]{2,1,0:T(8,128)} %bitcast.11), calls=%async_computation.3 | async-start | bytes 262144 | tf_op jit(solution)/shard_map/all_to_all | solution.py:81
  87.5 110.0 %all-reduce.5.cloned.1.call-start = ((), (), s32[]{:S(2)}) async-start(), calls=%async_computation.18 | async-start | bytes 524288 | tf_op jit(solution)/shard_map/psum | solution.py:62
  198.5 367.3 %copy-start.3 = (f32[512,128]{1,0:T(8,128)}, f32[512,128]{1,0:T(8,128)S(1)}, u32[]{:S(2)}) copy-start(f32[512,128]{1,0:T(8,128)S(1)} %get-tuple-element.22) | copy-start | bytes 786436
  199.7 12.9 %all-to-all-start.7 = ((bf16[16,2,128]{2,1,0:T(2,128)(2,1)}), bf16[16,2,128]{2,1,0:T(2,128)(2,1)S(1)}, u32[]{:S(2)}, u32[]{:S(2)}) async-start(bf16[16,2,128]{2,1,0:T(2,128)(2,1)} %bitcast.21), calls=%async_computation.7 | async-start | bytes 16384 | tf_op jit(solution)/shard_map/all_to_all | solution.py:69
  212.6 10.0 %all-to-all-start.6 = ((bf16[16,16,128]{2,1,0:T(8,128)(2,1)}), bf16[16,16,128]{2,1,0:T(8,128)(2,1)S(1)}, u32[]{:S(2)}, u32[]{:S(2)}) async-start(bf16[16,16,128]{2,1,0:T(8,128)(2,1)} %bitcast.19), calls=%async_computation.6 | async-start | bytes 131072 | tf_op jit(solution)/shard_map/all_to_all | solution.py:68
  222.5 18.5 %all-to-all-start.4 = ((f32[16,16,128]{2,1,0:T(8,128)}), f32[16,16,128]{2,1,0:T(8,128)S(1)}, u32[]{:S(2)}, u32[]{:S(2)}) async-start(f32[16,16,128]{2,1,0:T(8,128)} %fusion.21), calls=%async_computation.4 | async-start | bytes 262144 | tf_op jit(solution)/shard_map/all_to_all | solution.py:96
  244.7 10.8 %all-to-all-start.8 = ((bf16[16,16,128]{2,1,0:T(8,128)(2,1)}), bf16[16,16,128]{2,1,0:T(8,128)(2,1)S(1)}, u32[]{:S(2)}, u32[]{:S(2)}) async-start(bf16[16,16,128]{2,1,0:T(8,128)(2,1)} %bitcast.24), calls=%async_computation.8 | async-start | bytes 131072 | tf_op jit(solution)/shard_map/all_to_all | solution.py:72
  268.3 9.9 %all-to-all-start.11 = ((f32[16,2,128]{2,1,0:T(2,128)}), f32[16,2,128]{2,1,0:T(2,128)S(1)}, u32[]{:S(2)}, u32[]{:S(2)}) async-start(f32[16,2,128]{2,1,0:T(2,128)} %bitcast.34), calls=%async_computation.11 | async-start | bytes 32768 | tf_op jit(solution)/shard_map/all_to_all | solution.py:88
  278.2 13.3 %all-to-all-start.9 = ((f32[16,16,128]{2,1,0:T(8,128)}), f32[16,16,128]{2,1,0:T(8,128)S(1)}, u32[]{:S(2)}, u32[]{:S(2)}) async-start(f32[16,16,128]{2,1,0:T(8,128)} %bitcast.28), calls=%async_computation.9 | async-start | bytes 262144 | tf_op jit(solution)/shard_map/all_to_all | solution.py:81
  284.8 114.7 %all-reduce.7.cloned.1.call-start = ((), (), s32[]{:S(2)}) async-start(), calls=%async_computation.19 | async-start | bytes 524288 | tf_op jit(solution)/shard_map/psum | solution.py:62
  292.3 110.2 %all-to-all-start.10 = ((f32[16,16,128]{2,1,0:T(8,128)}), f32[16,16,128]{2,1,0:T(8,128)}, u32[]{:S(2)}, u32[]{:S(2)}) async-start(f32[16,16,128]{2,1,0:T(8,128)} %fusion.23), calls=%async_computation.10 | async-start | bytes 262144 | tf_op jit(solution)/shard_map/all_to_all | solution.py:96
  569.7 10.4 %all-to-all-start.13 = ((bf16[16,2,128]{2,1,0:T(2,128)(2,1)}), bf16[16,2,128]{2,1,0:T(2,128)(2,1)}, u32[]{:S(2)}, u32[]{:S(2)}) async-start(bf16[16,2,128]{2,1,0:T(2,128)(2,1)} %bitcast.38), calls=%async_computation.13 | async-start | bytes 16384 | tf_op jit(solution)/shard_map/all_to_all | solution.py:69
  580.2 10.7 %all-to-all-start.12 = ((bf16[16,16,128]{2,1,0:T(8,128)(2,1)}), bf16[16,16,128]{2,1,0:T(8,128)(2,1)}, u32[]{:S(2)}, u32[]{:S(2)}) async-start(bf16[16,16,128]{2,1,0:T(8,128)(2,1)} %bitcast.36), calls=%async_computation.12 | async-start | bytes 131072 | tf_op jit(solution)/shard_map/all_to_all | solution.py:68
  590.8 15.9 %all-to-all-start.14 = ((bf16[16,16,128]{2,1,0:T(8,128)(2,1)}), bf16[16,16,128]{2,1,0:T(8,128)(2,1)S(1)}, u32[]{:S(2)}, u32[]{:S(2)}) async-start(bf16[16,16,128]{2,1,0:T(8,128)(2,1)} %bitcast.41), calls=%async_computation.14 | async-start | bytes 131072 | tf_op jit(solution)/shard_map/all_to_all | solution.py:72
  619.5 10.1 %all-to-all-start.17 = ((f32[16,2,128]{2,1,0:T(2,128)}), f32[16,2,128]{2,1,0:T(2,128)S(1)}, u32[]{:S(2)}, u32[]{:S(2)}) async-start(f32[16,2,128]{2,1,0:T(2,128)} %bitcast.49), calls=%async_computation.17 | async-start | bytes 32768 | tf_op jit(solution)/shard_map/all_to_all | solution.py:88
  629.6 13.4 %all-to-all-start.15 = ((f32[16,16,128]{2,1,0:T(8,128)}), f32[16,16,128]{2,1,0:T(8,128)S(1)}, u32[]{:S(2)}, u32[]{:S(2)}) async-start(f32[16,16,128]{2,1,0:T(8,128)} %bitcast.44), calls=%async_computation.15 | async-start | bytes 262144 | tf_op jit(solution)/shard_map/all_to_all | solution.py:81
  636.2 116.6 %all-reduce.9.cloned.1.call-start = ((), (), s32[]{:S(2)}) async-start(), calls=%async_computation.20 | async-start | bytes 524288 | tf_op jit(solution)/shard_map/psum | solution.py:62
  640.4 198.6 %copy-start.7 = (f32[512,128]{1,0:T(8,128)S(1)}, f32[512,128]{1,0:T(8,128)}, u32[]{:S(2)}) copy-start(f32[512,128]{1,0:T(8,128)} %multiply_add_fusion.4) | copy-start | bytes 786436
  643.0 112.1 %all-to-all-start.16 = ((f32[16,16,128]{2,1,0:T(8,128)}), f32[16,16,128]{2,1,0:T(8,128)S(1)}, u32[]{:S(2)}, u32[]{:S(2)}) async-start(f32[16,16,128]{2,1,0:T(8,128)} %fusion.25), calls=%async_computation.16 | async-start | bytes 262144 | tf_op jit(solution)/shard_map/all_to_all | solution.py:96
  (21 other events, 1212.0 us)
Sparse Core Ops, SparseCore 0:
  91.3 106.1 all-reduce.4
  290.6 108.8 all-reduce.6
  642.2 110.5 all-reduce.8
where the time goes:
time: 858 us; the launch traced here: 847 us
  waiting for transfers between devices  334 us (39%)
  blocking collectives  228 us (27%)
  starting transfers between devices  109 us (13%)
  matrix products  62.6 us (7%)
  other arithmetic  46.5 us (5%)
  local copies, waits for them, and re-layouts  41.5 us (5%)
  between operations  26.4 us (3%)
    psum x3, waiting for transfers between devices, tube_total(): return lax.psum(partial_value, 'narrow')  295 us
    psum x2, blocking collectives, squares(): return lax.psum(local_inner(vector_set, vector_set), ('wide', 'narrow'))  150 us
    psum x1, blocking collectives, local(): lax.psum(local_inner(direction, image), ('wide', 'narrow'))  77.7 us
    dot_general x5, matrix products, model_values(): lax.dot_general(pairs, rows_second, (((1,), (1,)), ((), ())), preferred_e...  33.1 us
    all_to_all x3, starting transfers between devices, give_back(): lax.all_to_all(parts[1].reshape(narrow_count, slots_b, -1), 'narrow', spl...  26 us
    all_to_all x3, starting transfers between devices, fetch(): lax.all_to_all(send_b, 'narrow', split_axis=0, concat_axis=0, tiled=True)  22.6 us
    dot_general x3, local copies, waits for them, and re-layouts, transposed(): lax.dot_general(upstream, pairs, (((0,), (0,)), ((), ())), preferred_elem...  19.2 us
    all_to_all x3, starting transfers between devices, fetch(): lax.all_to_all(send_c, 'wide', split_axis=0, concat_axis=0, tiled=True)  18.2 us
  transfers between devices with their start and end apart: 21, of which 15 were waited for; matrix products, arithmetic and copies ran while one was open for 10% of the time, Pallas kernels for 0%

commit v1 on v0

--- a/solution.py
+++ b/solution.py
@@ -132,7 +132,7 @@
         )
 
     def squares(vector_set):
-        return lax.psum(local_inner(vector_set, vector_set), ("wide", "narrow"))
+        return lax.psum(lax.psum(local_inner(vector_set, vector_set), "wide"), "narrow")
 
     solution = (
         jnp.zeros_like(gradient[0]),

time: 858 us -> 909 us (1.059)
  blocking collectives: 228 us -> 277 us
    psum x1 -> x2, blocking collectives: 77.7 us -> 150 us  [local(): lax.psum(local_inner(direction, image), ('wide', 'narrow'))]
    psum x2 -> x4, blocking collectives: 150 us -> 127 us  [the longest x2 63.9 us: squares(): lax.psum(local_inner(vector_set, vector_set), 'wide')]
where the time goes in v1:
time: 909 us; the launch traced here: 898 us
  waiting for transfers between devices  334 us (37%)
  blocking collectives  277 us (30%)
  starting transfers between devices  110 us (12%)
  matrix products  62.6 us (7%)
  other arithmetic  46.6 us (5%)
  local copies, waits for them, and re-layouts  41.5 us (5%)
  between operations  26.4 us (3%)
    psum x3, waiting for transfers between devices, tube_total(): return lax.psum(partial_value, 'narrow')  295 us
    psum x2, blocking collectives, local(): lax.psum(local_inner(direction, image), ('wide', 'narrow'))  150 us
    psum x2, blocking collectives, squares(): lax.psum(local_inner(vector_set, vector_set), 'wide')  63.9 us
    psum x2, blocking collectives, squares(): lax.psum(lax.psum(local_inner(vector_set, vector_set), 'wide'), 'narrow')  63.2 us
    dot_general x5, matrix products, model_values(): lax.dot_general(pairs, rows_second, (((1,), (1,)), ((), ())), preferred_e...  33.1 us
    all_to_all x3, starting transfers between devices, give_back(): lax.all_to_all(parts[1].reshape(narrow_count, slots_b, -1), 'narrow', spl...  26 us
    all_to_all x3, starting transfers between devices, fetch(): lax.all_to_all(send_b, 'narrow', split_axis=0, concat_axis=0, tiled=True)  23.5 us
    dot_general x3, local copies, waits for them, and re-layouts, transposed(): lax.dot_general(upstream, pairs, (((0,), (0,)), ((), ())), preferred_elem...  19.2 us
  transfers between devices with their start and end apart: 21, of which 15 were waited for; matrix products, arithmetic and copies ran while one was open for 10% of the time, Pallas kernels for 0%

profile of v1, /device:TPU:1, one launch (start us, length us, event | category | flops | bytes accessed | tf_op | source)
XLA Modules:
  0.0 898.1 jit_solution(14947684089069232221)
XLA Ops:
  10.0 7.6 all-to-all-start.1
  18.9 7.4 broadcast_compare_fusion
  27.7 6.7 all-to-all-start
  40.9 11.1 %all-to-all-start.2 = ((bf16[16,16,128]{2,1,0:T(8,128)(2,1)}), bf16[16,16,128]{2,1,0:T(8,128)(2,1)S(1)}, u32[]{:S(2)}, u32[]{:S(2)}) async-start(bf16[16,16,128]{2,1,0:T(8,128)(2,1)} %bitcast.6), calls=%async_computation.2 | async-start | bytes 131072 | tf_op jit(solution)/shard_map/all_to_all | solution.py:72
  59.8 8.6 subtract_multiply_fusion
  89.6 6.4 copy.18
  98.0 99.5 %all-reduce.4.cloned.1.call-done = f32[512,128]{1,0:T(8,128)} async-done(((f32[512,128]{1,0:T(8,128)}), f32[512,128]{1,0:T(8,128)}) %all-reduce.4.cloned.1.call-update) | async-done | bytes 262160 | tf_op jit(solution)/shard_map/psum | solution.py:62
  199.7 6.5 all-to-all-start.7
  222.5 9.3 %all-to-all-start.4 = ((f32[16,16,128]{2,1,0:T(8,128)}), f32[16,16,128]{2,1,0:T(8,128)S(1)}, u32[]{:S(2)}, u32[]{:S(2)}) async-start(f32[16,16,128]{2,1,0:T(8,128)} %fusion.21), calls=%async_computation.4 | async-start | bytes 262144 | tf_op jit(solution)/shard_map/all_to_all | solution.py:96
  255.6 7.0 fusion.4
  278.2 6.6 all-to-all-start.9
  292.3 7.6 all-to-all-start.10
  302.3 97.3 %all-reduce.6.cloned.1.call-done = f32[512,128]{1,0:T(8,128)} async-done(((f32[512,128]{1,0:T(8,128)}), f32[512,128]{1,0:T(8,128)}) %all-reduce.6.cloned.1.call-update) | async-done | bytes 262160 | tf_op jit(solution)/shard_map/psum | solution.py:62
  407.0 33.6 %psum.64 = f32[]{:T(128)} all-reduce(f32[]{:T(128)S(6)} %add.169), channel_id=1, replica_groups=mesh['wide'=16,'narrow'=16] {'wide'}, use_global_device_ids=true, to_apply=%region_9.0 | all-reduce | flops 1 | bytes 8 | tf_op jit(solution)/shard_map/psum | solution.py:135
  441.9 31.4 %psum.65 = f32[]{:T(128)} all-reduce(f32[]{:T(128)} %psum.64), channel_id=1, replica_groups=mesh['wide'=16,'narrow'=16] {'narrow'}, use_global_device_ids=true, to_apply=%region_10.0 | all-reduce | flops 1 | bytes 8 | tf_op jit(solution)/shard_map/psum | solution.py:135
  473.3 72.7 %psum.67 = f32[]{:T(128)} all-reduce(f32[]{:T(128)S(6)} %add.174), channel_id=1, replica_groups=mesh['wide'=16,'narrow'=16] {'wide','narrow'}, use_global_device_ids=true, to_apply=%region_20.0 | all-reduce | flops 1 | bytes 8 | tf_op jit(solution)/shard_map/psum | solution.py:156
  552.2 30.3 %psum.68 = f32[]{:T(128)} all-reduce(f32[]{:T(128)S(6)} %add.179), channel_id=1, replica_groups=mesh['wide'=16,'narrow'=16] {'wide'}, use_global_device_ids=true, to_apply=%region_24.0 | all-reduce | flops 1 | bytes 8 | tf_op jit(solution)/shard_map/psum | solution.py:135
  582.5 31.7 %psum.69 = f32[]{:T(128)} all-reduce(f32[]{:T(128)} %psum.68), channel_id=1, replica_groups=mesh['wide'=16,'narrow'=16] {'narrow'}, use_global_device_ids=true, to_apply=%region_25.0 | all-reduce | flops 1 | bytes 8 | tf_op jit(solution)/shard_map/psum | solution.py:135
  640.6 8.7 all-to-all-start.14
  657.4 7.0 fusion.5
  680.2 6.6 all-to-all-start.15
  693.7 9.1 %all-to-all-start.16 = ((f32[16,16,128]{2,1,0:T(8,128)}), f32[16,16,128]{2,1,0:T(8,128)S(1)}, u32[]{:S(2)}, u32[]{:S(2)}) async-start(f32[16,16,128]{2,1,0:T(8,128)} %fusion.25), calls=%async_computation.16 | async-start | bytes 262144 | tf_op jit(solution)/shard_map/all_to_all | solution.py:96
  705.5 98.0 %all-reduce.8.cloned.1.call-done = f32[512,128]{1,0:T(8,128)} async-done(((f32[512,128]{1,0:T(8,128)}), f32[512,128]{1,0:T(8,128)}) %all-reduce.8.cloned.1.call-update) | async-done | bytes 262160 | tf_op jit(solution)/shard_map/psum | solution.py:62
  809.9 77.7 %psum.71 = f32[]{:T(128)} all-reduce(f32[]{:T(128)S(6)} %add.187), channel_id=1, replica_groups=mesh['wide'=16,'narrow'=16] {'wide','narrow'}, use_global_device_ids=true, to_apply=%region_35.0 | all-reduce | flops 1 | bytes 8 | tf_op jit(solution)/shard_map/psum | solution.py:156
  (147 shorter events, 183.3 us)
Async XLA Ops:
  10.0 17.7 %all-to-all-start.1 = ((bf16[16,2,128]{2,1,0:T(2,128)(2,1)}), bf16[16,2,128]{2,1,0:T(2,128)(2,1)S(1)}, u32[]{:S(2)}, u32[]{:S(2)}) async-start(bf16[16,2,128]{2,1,0:T(2,128)(2,1)} %bitcast.3), calls=%async_computation.1 | async-start | bytes 16384 | tf_op jit(solution)/shard_map/all_to_all | solution.py:69
  27.7 13.2 %all-to-all-start = ((bf16[16,16,128]{2,1,0:T(8,128)(2,1)}), bf16[16,16,128]{2,1,0:T(8,128)(2,1)S(1)}, u32[]{:S(2)}, u32[]{:S(2)}) async-start(bf16[16,16,128]{2,1,0:T(8,128)(2,1)} %bitcast.1), calls=%async_computation | async-start | bytes 131072 | tf_op jit(solution)/shard_map/all_to_all | solution.py:68
  40.9 19.0 %all-to-all-start.2 = ((bf16[16,16,128]{2,1,0:T(8,128)(2,1)}), bf16[16,16,128]{2,1,0:T(8,128)(2,1)S(1)}, u32[]{:S(2)}, u32[]{:S(2)}) async-start(bf16[16,16,128]{2,1,0:T(8,128)(2,1)} %bitcast.6), calls=%async_computation.2 | async-start | bytes 131072 | tf_op jit(solution)/shard_map/all_to_all | solution.py:72
  59.8 202.8 %copy-start.10 = (bf16[16,16,128]{2,1,0:T(8,128)(2,1)}, bf16[16,16,128]{2,1,0:T(8,128)(2,1)S(1)}, u32[]{:S(2)}) copy-start(bf16[16,16,128]{2,1,0:T(8,128)(2,1)S(1)} %all-to-all-done.2) | copy-start | bytes 196612
  74.1 9.9 %all-to-all-start.5 = ((f32[16,2,128]{2,1,0:T(2,128)}), f32[16,2,128]{2,1,0:T(2,128)S(1)}, u32[]{:S(2)}, u32[]{:S(2)}) async-start(f32[16,2,128]{2,1,0:T(2,128)} %bitcast.17), calls=%async_computation.5 | async-start | bytes 32768 | tf_op jit(solution)/shard_map/all_to_all | solution.py:88
  84.0 11.9 %all-to-all-start.3 = ((f32[16,16,128]{2,1,0:T(8,128)}), f32[16,16,128]{2,1,0:T(8,128)S(1)}, u32[]{:S(2)}, u32[]{:S(2)}) async-start(f32[16,16,128]{2,1,0:T(8,128)} %bitcast.11), calls=%async_computation.3 | async-start | bytes 262144 | tf_op jit(solution)/shard_map/all_to_all | solution.py:81
  87.5 110.0 %all-reduce.4.cloned.1.call-start = ((), (), s32[]{:S(2)}) async-start(), calls=%async_computation.18 | async-start | bytes 524288 | tf_op jit(solution)/shard_map/psum | solution.py:62
  198.5 417.0 %copy-start.3 = (f32[512,128]{1,0:T(8,128)}, f32[512,128]{1,0:T(8,128)S(1)}, u32[]{:S(2)}) copy-start(f32[512,128]{1,0:T(8,128)S(1)} %get-tuple-element.20) | copy-start | bytes 786436
  199.7 12.9 %all-to-all-start.7 = ((bf16[16,2,128]{2,1,0:T(2,128)(2,1)}), bf16[16,2,128]{2,1,0:T(2,128)(2,1)S(1)}, u32[]{:S(2)}, u32[]{:S(2)}) async-start(bf16[16,2,128]{2,1,0:T(2,128)(2,1)} %bitcast.21), calls=%async_computation.7 | async-start | bytes 16384 | tf_op jit(solution)/shard_map/all_to_all | solution.py:69
  212.6 10.0 %all-to-all-start.6 = ((bf16[16,16,128]{2,1,0:T(8,128)(2,1)}), bf16[16,16,128]{2,1,0:T(8,128)(2,1)S(1)}, u32[]{:S(2)}, u32[]{:S(2)}) async-start(bf16[16,16,128]{2,1,0:T(8,128)(2,1)} %bitcast.19), calls=%async_computation.6 | async-start | bytes 131072 | tf_op jit(solution)/shard_map/all_to_all | solution.py:68
  222.5 18.5 %all-to-all-start.4 = ((f32[16,16,128]{2,1,0:T(8,128)}), f32[16,16,128]{2,1,0:T(8,128)S(1)}, u32[]{:S(2)}, u32[]{:S(2)}) async-start(f32[16,16,128]{2,1,0:T(8,128)} %fusion.21), calls=%async_computation.4 | async-start | bytes 262144 | tf_op jit(solution)/shard_map/all_to_all | solution.py:96
  244.7 10.8 %all-to-all-start.8 = ((bf16[16,16,128]{2,1,0:T(8,128)(2,1)}), bf16[16,16,128]{2,1,0:T(8,128)(2,1)S(1)}, u32[]{:S(2)}, u32[]{:S(2)}) async-start(bf16[16,16,128]{2,1,0:T(8,128)(2,1)} %bitcast.24), calls=%async_computation.8 | async-start | bytes 131072 | tf_op jit(solution)/shard_map/all_to_all | solution.py:72
  268.3 9.9 %all-to-all-start.11 = ((f32[16,2,128]{2,1,0:T(2,128)}), f32[16,2,128]{2,1,0:T(2,128)S(1)}, u32[]{:S(2)}, u32[]{:S(2)}) async-start(f32[16,2,128]{2,1,0:T(2,128)} %bitcast.34), calls=%async_computation.11 | async-start | bytes 32768 | tf_op jit(solution)/shard_map/all_to_all | solution.py:88
  278.2 13.3 %all-to-all-start.9 = ((f32[16,16,128]{2,1,0:T(8,128)}), f32[16,16,128]{2,1,0:T(8,128)S(1)}, u32[]{:S(2)}, u32[]{:S(2)}) async-start(f32[16,16,128]{2,1,0:T(8,128)} %bitcast.28), calls=%async_computation.9 | async-start | bytes 262144 | tf_op jit(solution)/shard_map/all_to_all | solution.py:81
  284.8 114.7 %all-reduce.6.cloned.1.call-start = ((), (), s32[]{:S(2)}) async-start(), calls=%async_computation.19 | async-start | bytes 524288 | tf_op jit(solution)/shard_map/psum | solution.py:62
  292.3 109.6 %all-to-all-start.10 = ((f32[16,16,128]{2,1,0:T(8,128)}), f32[16,16,128]{2,1,0:T(8,128)}, u32[]{:S(2)}, u32[]{:S(2)}) async-start(f32[16,16,128]{2,1,0:T(8,128)} %fusion.23), calls=%async_computation.10 | async-start | bytes 262144 | tf_op jit(solution)/shard_map/all_to_all | solution.py:96
  619.5 10.4 %all-to-all-start.13 = ((bf16[16,2,128]{2,1,0:T(2,128)(2,1)}), bf16[16,2,128]{2,1,0:T(2,128)(2,1)}, u32[]{:S(2)}, u32[]{:S(2)}) async-start(bf16[16,2,128]{2,1,0:T(2,128)(2,1)} %bitcast.38), calls=%async_computation.13 | async-start | bytes 16384 | tf_op jit(solution)/shard_map/all_to_all | solution.py:69
  629.9 10.7 %all-to-all-start.12 = ((bf16[16,16,128]{2,1,0:T(8,128)(2,1)}), bf16[16,16,128]{2,1,0:T(8,128)(2,1)}, u32[]{:S(2)}, u32[]{:S(2)}) async-start(bf16[16,16,128]{2,1,0:T(8,128)(2,1)} %bitcast.36), calls=%async_computation.12 | async-start | bytes 131072 | tf_op jit(solution)/shard_map/all_to_all | solution.py:68
  640.6 16.8 %all-to-all-start.14 = ((bf16[16,16,128]{2,1,0:T(8,128)(2,1)}), bf16[16,16,128]{2,1,0:T(8,128)(2,1)S(1)}, u32[]{:S(2)}, u32[]{:S(2)}) async-start(bf16[16,16,128]{2,1,0:T(8,128)(2,1)} %bitcast.41), calls=%async_computation.14 | async-start | bytes 131072 | tf_op jit(solution)/shard_map/all_to_all | solution.py:72
  670.1 10.1 %all-to-all-start.17 = ((f32[16,2,128]{2,1,0:T(2,128)}), f32[16,2,128]{2,1,0:T(2,128)S(1)}, u32[]{:S(2)}, u32[]{:S(2)}) async-start(f32[16,2,128]{2,1,0:T(2,128)} %bitcast.49), calls=%async_computation.17 | async-start | bytes 32768 | tf_op jit(solution)/shard_map/all_to_all | solution.py:88
  680.2 13.4 %all-to-all-start.15 = ((f32[16,16,128]{2,1,0:T(8,128)}), f32[16,16,128]{2,1,0:T(8,128)S(1)}, u32[]{:S(2)}, u32[]{:S(2)}) async-start(f32[16,16,128]{2,1,0:T(8,128)} %bitcast.44), calls=%async_computation.15 | async-start | bytes 262144 | tf_op jit(solution)/shard_map/all_to_all | solution.py:81
  686.9 116.6 %all-reduce.8.cloned.1.call-start = ((), (), s32[]{:S(2)}) async-start(), calls=%async_computation.20 | async-start | bytes 524288 | tf_op jit(solution)/shard_map/psum | solution.py:62
  691.1 198.6 %copy-start.7 = (f32[512,128]{1,0:T(8,128)S(1)}, f32[512,128]{1,0:T(8,128)}, u32[]{:S(2)}) copy-start(f32[512,128]{1,0:T(8,128)} %multiply_add_fusion.4) | copy-start | bytes 786436
  693.7 112.1 %all-to-all-start.16 = ((f32[16,16,128]{2,1,0:T(8,128)}), f32[16,16,128]{2,1,0:T(8,128)S(1)}, u32[]{:S(2)}, u32[]{:S(2)}) async-start(f32[16,16,128]{2,1,0:T(8,128)} %fusion.25), calls=%async_computation.16 | async-start | bytes 262144 | tf_op jit(solution)/shard_map/all_to_all | solution.py:96
  (21 other events, 1212.9 us)
Sparse Core Ops, SparseCore 0:
  91.3 106.1 all-reduce.3
  290.6 108.8 all-reduce.5
  692.8 110.5 all-reduce.7
